TPU v7x, 32 devices: a whole 2x2x4 slice. The times are simulated.
32 devices in a mesh: psg: 32 (over z, y, x, core), qry: 1.
Axes of the slice: x: 2, y: 2, z: 4, core: 2. Of those that a mesh axis runs over, the one named last changes fastest.
Arguments:
- queries: bfloat16 [1024, 4096], P('psg', 'qry'), may hold values from -6 to 6
- grad_out: bfloat16 [1024, 4096], P('psg', 'qry'), may hold values from -6 to 6
- attn_out: bfloat16 [1024, 4096], P('psg', 'qry'), may hold values from -6 to 6
- log_sum: float32 [32, 1024], P('qry', 'psg'), may hold values from 3 to 5
- keys: bfloat16 [16384, 1024], P('psg', 'qry'), may hold values from -6 to 6
- values: bfloat16 [16384, 1024], P('psg', 'qry'), may hold values from -6 to 6
- proj_weight: bfloat16 [4096, 4096], P('psg', 'qry'), may hold values from -0.09375 to 0.09375
- attend: int32 [4, 16], replicated, may hold values from 0 to 31, all different within a row; in each aligned block of 4 rows (0 to 3, 4 to 7, ...) at most 4 rows name the same one
- qlen: int32 [4], replicated, may hold values from 128 to 256, as said below
Outputs:
- grad_query: float32 [1024, 4096], P('psg', 'qry')
- grad_keys: float32 [16384, 1024], P('psg', 'qry')
- grad_values: float32 [16384, 1024], P('psg', 'qry')
- grad_hidden: float32 [1024, 4096], P('psg')
Inputs may be any that keep to these rules, and one draw needn't show every extreme that they name: `attend`: each question names 16 different blocks; each block is named by at least one question and at most 4, and some block by exactly 4. `qlen`: each a multiple of 128; some question has 256 rows.
All inputs are finite; a program needn't handle non-finite values.
Results may differ from a plain program's by a relative error of at most 0.0049.
Values may be sent and summed in bfloat16 or wider, within the bound.
A program may use at most 128 MiB of HBM per device.

v0:
```python
import functools

import jax
import jax.numpy as jnp
from jax import lax
from jax.experimental import pallas as pl
from jax.experimental.pallas import tpu as pltpu
from jax.sharding import PartitionSpec as P

ATTN_WIDTH = 128
GROUP = 4
PADDED_ASK_LEN = 256
TILE = 128
LOG2_E = 1.4426950408889634
SCALE = ATTN_WIDTH ** (-0.5)
NT = (((1,), (1,)), ((), ()))
NN = (((1,), (0,)), ((), ()))


def dot(a, b, dims=NN):
    return lax.dot_general(a, b, dims, preferred_element_type=jnp.float32)


def head_rows(qg_ref, first, per_part, which):
    pieces = [
        qg_ref[first + k, which, :, h * ATTN_WIDTH : (h + 1) * ATTN_WIDTH]
        for k in range(per_part)
        for h in range(GROUP)
    ]
    return jnp.concatenate(pieces, axis=0)


def attention_kernel(
    blocks, tile_count, per_tile, attend, qlen, kv_ref, qg_ref, ld_ref, dkv_ref, dq_ref, dk_acc, dv_acc, dq_acc
):
    block = pl.program_id(0)
    per_part = per_tile // 2
    row_count = TILE // per_tile
    wide = GROUP * row_count

    @pl.when(block == 0)
    def _():
        dq_acc[...] = jnp.zeros_like(dq_acc)

    dk_acc[...] = jnp.zeros_like(dk_acc)
    dv_acc[...] = jnp.zeros_like(dv_acc)
    key_rows_t = kv_ref[0, 0].T

    def visit(tile, carry):
        keys, values = kv_ref[0, 0], kv_ref[0, 1]
        dk, dv = None, None
        for part in range(2):
            rows = slice(part * 256, part * 256 + 256)
            first = tile * per_tile + part * per_part
            q = head_rows(qg_ref, first, per_part, 0)
            g = head_rows(qg_ref, first, per_part, 1)
            ld = jnp.concatenate([ld_ref[first + k] for k in range(per_part)], axis=1)
            lse, delta = ld[0:1], ld[1:2]
            prob = jnp.exp2(dot(keys, q, NT) * (SCALE * LOG2_E) - lse)
            dprob = dot(values, g, NT)
            dscore = (prob * (dprob - delta)).astype(jnp.bfloat16)
            v_term = dot(prob.astype(jnp.bfloat16), g)
            k_term = dot(dscore, q)
            dv = v_term if dv is None else dv + v_term
            dk = k_term if dk is None else dk + k_term
            dq_acc[tile, :, rows] += dot(key_rows_t, dscore)
        dk_acc[...] += dk
        dv_acc[...] += dv
        return carry

    mine = lax.axis_index("psg")
    mine = mine - lax.rem(mine, blocks) + block
    questions, named = attend.shape

    def ask(question, carry):
        hits = attend[question, 0] == mine
        for i in range(1, named):
            hits = hits | (attend[question, i] == mine)
        first = question * (PADDED_ASK_LEN // TILE)
        count = jnp.where(hits, qlen[question] // TILE, 0)
        return lax.fori_loop(first, first + count, visit, carry)

    lax.fori_loop(0, questions, ask, 0)
    dkv_ref[0, 0] = (dk_acc[...] * SCALE).astype(dkv_ref.dtype)
    dkv_ref[0, 1] = dv_acc[...].astype(dkv_ref.dtype)

    @pl.when(block == blocks - 1)
    def _():
        def put(tile, carry):
            for k in range(per_tile):
                piece = dq_acc[tile, :, k * wide : (k + 1) * wide] * SCALE
                piece = piece.T.astype(dq_ref.dtype)
                for h in range(GROUP):
                    cols = slice(h * ATTN_WIDTH, (h + 1) * ATTN_WIDTH)
                    dq_ref[tile * per_tile + k, :, cols] = piece[h * row_count : (h + 1) * row_count]
            return carry

        lax.fori_loop(0, tile_count, put, 0)


def attention(attend, qlen, kv, qg, ld, out_dtype):
    blocks, _, span, width = kv.shape
    sources, _, row_count, lanes = qg.shape
    per_tile = TILE // row_count
    tile_count = sources // per_tile
    whole = lambda shape: pl.BlockSpec(shape, lambda b, *_: (0,) * len(shape))
    return pl.pallas_call(
        functools.partial(attention_kernel, blocks, tile_count, per_tile),
        out_shape=(
            jax.ShapeDtypeStruct(kv.shape, out_dtype),
            jax.ShapeDtypeStruct((sources, row_count, lanes), jnp.bfloat16),
        ),
        grid_spec=pltpu.PrefetchScalarGridSpec(
            num_scalar_prefetch=2,
            grid=(blocks,),
            in_specs=[
                pl.BlockSpec((1, 2, span, width), lambda b, *_: (b, 0, 0, 0)),
                whole(qg.shape),
                whole(ld.shape),
            ],
            out_specs=(
                pl.BlockSpec((1, 2, span, width), lambda b, *_: (b, 0, 0, 0)),
                whole((sources, row_count, lanes)),
            ),
            scratch_shapes=[
                pltpu.VMEM((span, width), jnp.float32),
                pltpu.VMEM((span, width), jnp.float32),
                pltpu.VMEM((tile_count, width, lanes), jnp.float32),
            ],
        ),
        compiler_params=pltpu.CompilerParams(vmem_limit_bytes=58 * 2**20),
        cost_estimate=pl.CostEstimate(
            flops=2 * blocks * span * width * lanes * tile_count * 5 // 2,
            bytes_accessed=16 * 2**20,
            transcendentals=blocks * span * lanes * tile_count // 2,
        ),
        name="attention",
    )(attend, qlen, kv, qg, ld)


def routes(kind, devices, slices, me):
    layers = devices // slices
    j, z = lax.rem(me, slices), me // slices
    base = me - j
    if kind in ("all", "cast"):

        def step(r):
            target = lax.rem(me + r, devices)
            return target, (target if kind == "all" else lax.rem(target, slices)), me

        return devices, step
    if kind == "layer":

        def step(r):
            other = lax.rem(j + r, slices)
            return base + other, other, j

        return slices, step
    if kind == "z":

        def step(r):
            other = lax.rem(z + r, layers)
            return other * slices + j, other, z

        return layers, step
    quads = slices // 2

    def step(r):
        other = lax.rem(j // 2 + r, quads)
        return base + 2 * other + lax.rem(j, 2), other, j // 2

    return quads, step


def repeat(first, count, body):
    if count - first <= 8:
        for r in range(first, count):
            body(r)
    else:
        lax.fori_loop(first, count, lambda r, c: (body(r), c)[1], 0)


def exchange_kernel(kinds, devices, slices, gathered, *refs):
    n = len(kinds)
    total = n + gathered
    sources, outs = refs[:total], refs[total : 2 * total]
    sems = refs[2 * total :]
    me = lax.axis_index("psg")
    barrier = pltpu.get_barrier_semaphore()
    if "all" in kinds or "cast" in kinds:
        greeted = ("all",)
    else:
        greeted = ("z", "layer")
    count = 0
    for kind in greeted:
        size, step = routes(kind, devices, slices, me)
        count += size - 1

        def greet(r, step=step):
            pl.semaphore_signal(barrier, inc=1, device_id={"psg": step(r)[0]}, device_id_type=pl.DeviceIdType.MESH)

        repeat(1, size, greet)
    pl.semaphore_wait(barrier, count)

    def remote(src, dst, send, recv, target):
        return pltpu.make_async_remote_copy(
            src_ref=src,
            dst_ref=dst,
            send_sem=send,
            recv_sem=recv,
            device_id={"psg": target},
            device_id_type=pl.DeviceIdType.MESH,
        )

    if gathered:
        j, z = lax.rem(me, slices), me // slices
        parity = lax.rem(j, 2)
        partner = me + 1 - 2 * parity
        layers = devices // slices
        mine, pair = sources[n], outs[n]
        send, recv, pair_send, pair_recv, own = sems[3 * n :]
        along = []
        for r in range(1, layers):
            target = lax.rem(z + r, layers) * slices + j
            along.append(remote(mine, pair.at[parity, z], send.at[r], recv.at[r], target))
            along[-1].start()
        across = [remote(mine, pair.at[parity, z], pair_send.at[0], pair_recv.at[0], partner)]
        across[0].start()
        kept = pltpu.make_async_copy(mine, pair.at[parity, z], own)
        kept.start()

    moves, stays = [], []
    for i, kind in enumerate(kinds):
        size, step = routes(kind, devices, slices, me)

        def copy(r, i=i, step=step):
            target, chunk, slot = step(r)
            return remote(
                sources[i].at[chunk], outs[i].at[slot], sems[3 * i].at[r], sems[3 * i + 1].at[r], target
            )

        moves.append((size, copy))
        chunk, slot = step(0)[1:]
        stays.append(pltpu.make_async_copy(sources[i].at[chunk], outs[i].at[slot], sems[3 * i + 2]))
    for size, copy in moves:
        repeat(1, size, lambda r, copy=copy: copy(r).start())
    for stay in stays:
        stay.start()

    if gathered:
        for r in range(1, layers):
            along[r - 1].wait_recv()
            landed = pair.at[parity, lax.rem(z - r + layers, layers)]
            across.append(remote(landed, landed, pair_send.at[r], pair_recv.at[r], partner))
            across[-1].start()
        for copy in along:
            copy.wait_send()
        for copy in across:
            copy.wait()
        kept.wait()
    for stay in stays:
        stay.wait()
    for size, copy in moves:
        repeat(1, size, lambda r, copy=copy: copy(r).wait())


def exchange(name, number, devices, slices, parts, gather=None):
    kinds = tuple(kind for kind, _ in parts)
    arrays = [array for _, array in parts]
    layers = devices // slices
    sizes = {"all": devices, "cast": devices, "layer": slices, "z": layers, "parity": slices // 2}
    shapes = [
        jax.ShapeDtypeStruct((sizes[kind],) + array.shape[1:], array.dtype) for kind, array in parts
    ]
    scratch = []
    for kind in kinds:
        scratch += [pltpu.SemaphoreType.DMA((sizes[kind],))] * 2 + [pltpu.SemaphoreType.DMA]
    if gather is not None:
        arrays.append(gather)
        shapes.append(jax.ShapeDtypeStruct((2, layers) + gather.shape, gather.dtype))
        scratch += [pltpu.SemaphoreType.DMA((layers,))] * 4 + [pltpu.SemaphoreType.DMA]
    anywhere = pl.BlockSpec(memory_space=pl.ANY)
    return pl.pallas_call(
        functools.partial(exchange_kernel, kinds, devices, slices, int(gather is not None)),
        out_shape=tuple(shapes),
        in_specs=[anywhere] * len(arrays),
        out_specs=tuple([anywhere] * len(shapes)),
        scratch_shapes=scratch,
        compiler_params=pltpu.CompilerParams(collective_id=number, has_side_effects=True),
        cost_estimate=pl.CostEstimate(flops=0, bytes_accessed=60 * 2**20, transcendentals=0),
        name=name,
    )(*arrays)


def send_to(src, dst, send, recv, target):
    return pltpu.make_async_remote_copy(
        src_ref=src,
        dst_ref=dst,
        send_sem=send,
        recv_sem=recv,
        device_id={"psg": target},
        device_id_type=pl.DeviceIdType.MESH,
    )


def inward_kernel(devices, slices, *refs):
    q_ref, g_ref, ld_ref, k_ref, v_ref, qg_out, ld_out, kv_out = refs[:8]
    in_send, in_recv, kv_send, kv_recv, ld_send, ld_recv, up_send, up_recv, down_send, down_recv, own = refs[8:]
    layers = devices // slices
    me = lax.axis_index("psg")
    j, z = lax.rem(me, slices), me // slices
    base = me - j
    lanes, width = q_ref.shape[1] // slices, k_ref.shape[1] // slices
    barrier = pltpu.get_barrier_semaphore()

    def greet(r, c):
        other = lax.rem(me + r, devices)
        pl.semaphore_signal(barrier, inc=1, device_id={"psg": other}, device_id_type=pl.DeviceIdType.MESH)
        return c

    lax.fori_loop(1, devices, greet, 0)
    pl.semaphore_wait(barrier, devices - 1)

    def columns(ref, part, size):
        return ref.at[:, pl.ds(pl.multiple_of(part * size, size), size)]

    def inside(r):
        other = lax.rem(j + r, slices)
        return [
            send_to(columns(ref, other, lanes), qg_out.at[me, i], in_send.at[i, r], in_recv.at[i, r], base + other)
            for i, ref in enumerate((q_ref, g_ref))
        ]

    def passages(r):
        other = lax.rem(j + r, slices)
        return [
            send_to(columns(ref, other, width), kv_out.at[j, i], kv_send.at[i, r], kv_recv.at[i, r], base + other)
            for i, ref in enumerate((k_ref, v_ref))
        ]

    def small(r):
        other = lax.rem(me + r, devices)
        return send_to(ld_ref.at[lax.rem(other, slices)], ld_out.at[me], ld_send.at[r], ld_recv.at[r], other)

    def hop(sent, r, up):
        layer = z - sent if up else z + sent
        source = layer * slices + lax.rem(j - r + slices, slices)
        ref = qg_out.at[source]
        if up:
            return send_to(ref, ref, up_send.at[sent, r], up_recv.at[sent, r], me + slices)
        return send_to(ref, ref, down_send.at[sent, r], down_recv.at[sent, r], me - slices)

    def hop_here(sent, r, up):
        layer = z - sent - 1 if up else z + sent + 1
        source = layer * slices + lax.rem(j - r + slices, slices)
        ref = qg_out.at[source]
        if up:
            return send_to(ref, ref, up_send.at[sent, r], up_recv.at[sent, r], lax.rem(me + 1, devices))
        return send_to(ref, ref, down_send.at[sent, r], down_recv.at[sent, r], lax.rem(me + 1, devices))

    kept = [
        pltpu.make_async_copy(columns(q_ref, j, lanes), qg_out.at[me, 0], own.at[0]),
        pltpu.make_async_copy(columns(g_ref, j, lanes), qg_out.at[me, 1], own.at[1]),
        pltpu.make_async_copy(columns(k_ref, j, width), kv_out.at[j, 0], own.at[2]),
        pltpu.make_async_copy(columns(v_ref, j, width), kv_out.at[j, 1], own.at[3]),
        pltpu.make_async_copy(ld_ref.at[j], ld_out.at[me], own.at[4]),
    ]
    for copy in kept:
        copy.start()
    for r in range(1, slices):
        for copy in inside(r):
            copy.start()
    for r in range(1, slices):
        for copy in passages(r):
            copy.start()
    for copy in kept:
        copy.wait()

    def forward(sent, r):
        @pl.when((z < layers - 1) & (z >= sent))
        def _():
            hop(sent, r, True).start()

        @pl.when((z > 0) & (z + sent < layers))
        def _():
            hop(sent, r, False).start()

    forward(0, 0)

    def first(r, c):
        for copy in inside(r):
            copy.wait_recv()
        forward(0, r)
        return c

    lax.fori_loop(1, slices, first, 0)
    lax.fori_loop(1, devices, lambda r, c: (small(r).start(), c)[1], 0)

    def later(n, c):
        sent, r = n // slices, lax.rem(n, slices)

        @pl.when(z > sent)
        def _():
            hop_here(sent, r, True).wait_recv()

        @pl.when((z > sent) & (z < layers - 1))
        def _():
            hop(sent + 1, r, True).start()

        @pl.when(z + sent + 1 < layers)
        def _():
            hop_here(sent, r, False).wait_recv()

        @pl.when((z + sent + 1 < layers) & (z > 0))
        def _():
            hop(sent + 1, r, False).start()

        return c

    lax.fori_loop(0, (layers - 1) * slices, later, 0)

    for r in range(1, slices):
        for copy in inside(r):
            copy.wait_send()
        for copy in passages(r):
            copy.wait()
    lax.fori_loop(1, devices, lambda r, c: (small(r).wait(), c)[1], 0)

    def ended(n, c):
        sent, r = n // slices, lax.rem(n, slices)

        @pl.when((z < layers - 1) & (z >= sent))
        def _():
            hop(sent, r, True).wait_send()

        @pl.when((z > 0) & (z + sent < layers))
        def _():
            hop(sent, r, False).wait_send()

        return c

    lax.fori_loop(0, (layers - 1) * slices, ended, 0)


def inward(devices, slices, queries, grad_out, ld, keys, values):
    layers = devices // slices
    row_count, columns = queries.shape
    span = keys.shape[0]
    dma = pltpu.SemaphoreType.DMA
    anywhere = pl.BlockSpec(memory_space=pl.ANY)
    return pl.pallas_call(
        functools.partial(inward_kernel, devices, slices),
        out_shape=(
            jax.ShapeDtypeStruct((devices, 2, row_count, columns // slices), queries.dtype),
            jax.ShapeDtypeStruct((devices,) + ld.shape[1:], ld.dtype),
            jax.ShapeDtypeStruct((slices, 2, span, keys.shape[1] // slices), keys.dtype),
        ),
        in_specs=[anywhere] * 5,
        out_specs=(anywhere,) * 3,
        scratch_shapes=[dma((2, slices))] * 4
        + [dma((devices,))] * 2
        + [dma((layers, slices))] * 4
        + [dma((5,))],
        compiler_params=pltpu.CompilerParams(collective_id=0, has_side_effects=True),
        cost_estimate=pl.CostEstimate(flops=0, bytes_accessed=60 * 2**20, transcendentals=0),
        name="exchange_in",
    )(queries, grad_out, ld, keys, values)


def outward_kernel(devices, slices, dq_ref, dkv_ref, w_ref, gq_out, dkv_out, hid_out, *scratch):
    terms, summed, pair, weight, hidden = scratch[:5]
    term_send, term_recv, up_send, up_recv, down_send, down_recv, pair_send, pair_recv = scratch[5:13]
    w_send, w_recv, dkv_send, dkv_recv, gq_send, gq_recv, hid_send, hid_recv, own = scratch[13:]
    layers = devices // slices
    quads = slices // 2
    me = lax.axis_index("psg")
    j, z = lax.rem(me, slices), me // slices
    base = me - j
    parity = lax.rem(j, 2)
    partner = me + 1 - 2 * parity
    row_count, lanes = dq_ref.shape[2:]
    chunk_rows = 2 * row_count
    barrier = pltpu.get_barrier_semaphore()

    def greet(r, c):
        other = lax.rem(me + r, devices)
        pl.semaphore_signal(barrier, inc=1, device_id={"psg": other}, device_id_type=pl.DeviceIdType.MESH)
        return c

    lax.fori_loop(1, devices, greet, 0)
    pl.semaphore_wait(barrier, devices - 1)

    def term(c, r, here=False):
        other = lax.rem(z + r, layers)
        slot = lax.rem(z - r + layers, layers) if here else z
        devs = slice(2 * c, 2 * c + 2)
        return send_to(
            dq_ref.at[other, devs], terms.at[slot, devs], term_send.at[c, r], term_recv.at[c, r],
            other * slices + j,
        )

    def weights(r):
        other = lax.rem(j // 2 + r, quads)
        width = 2 * lanes
        source = w_ref.at[:, pl.ds(pl.multiple_of(other * width, width), width)]
        if r == 0:
            return pltpu.make_async_copy(source, weight.at[j // 2], own.at[0])
        return send_to(
            source, weight.at[j // 2], w_send.at[r], w_recv.at[r], base + 2 * other + parity
        )

    def passages(r):
        other = lax.rem(j + r, slices)
        if r == 0:
            return pltpu.make_async_copy(dkv_ref.at[other], dkv_out.at[j], own.at[1])
        return send_to(dkv_ref.at[other], dkv_out.at[j], dkv_send.at[r], dkv_recv.at[r], base + other)

    def rows(r):
        other = lax.rem(j + r, slices)
        if r == 0:
            return pltpu.make_async_copy(summed.at[other], gq_out.at[j], own.at[2])
        return send_to(summed.at[other], gq_out.at[j], gq_send.at[r], gq_recv.at[r], base + other)

    def piece(core, layer, c):
        return pair.at[core, layer, c * chunk_rows : (c + 1) * chunk_rows]

    def hop(sent, c, up):
        ref = piece(parity, z - sent if up else z + sent, c)
        if up:
            return send_to(ref, ref, up_send.at[sent, c], up_recv.at[sent, c], me + slices)
        return send_to(ref, ref, down_send.at[sent, c], down_recv.at[sent, c], me - slices)

    def hop_here(sent, c, up):
        ref = piece(parity, z - sent - 1 if up else z + sent + 1, c)
        other = lax.rem(me + 1, devices)
        if up:
            return send_to(ref, ref, up_send.at[sent, c], up_recv.at[sent, c], other)
        return send_to(ref, ref, down_send.at[sent, c], down_recv.at[sent, c], other)

    def across(layer, c, here=False):
        ref = piece(1 - parity if here else parity, layer, c)
        return send_to(ref, ref, pair_send.at[layer, c], pair_recv.at[layer, c], partner)

    def columns(layer, r):
        other = lax.rem(j + r, slices)
        target = layer * slices + other
        step = lax.rem(target - me + devices, devices)
        return send_to(
            hidden.at[layer, other], hid_out.at[me], hid_send.at[step], hid_recv.at[step], target
        )

    def product(layer):
        for c in range(quads):
            across(layer, c, True).wait_recv()
        matrix = weight[...].reshape(-1, 2 * lanes)
        out = dot(pair[0, layer], matrix[:, :lanes], NT) + dot(pair[1, layer], matrix[:, lanes:], NT)
        hidden[layer] = out.astype(hidden.dtype).reshape(hidden.shape[1:])

    for c in range(quads):
        for r in range(1, layers):
            term(c, r).start()
    for r in range(quads):
        weights(r).start()
    for r in range(slices):
        passages(r).start()

    for c in range(quads):
        devs = slice(2 * c, 2 * c + 2)
        total = dq_ref[z, devs].astype(jnp.float32)
        for r in range(1, layers):
            term(c, r, True).wait_recv()
            total += terms[lax.rem(z - r + layers, layers), devs].astype(jnp.float32)
        summed[devs] = total
        pair[parity, z, c * chunk_rows : (c + 1) * chunk_rows] = total.astype(pair.dtype).reshape(
            chunk_rows, lanes
        )

        @pl.when(z < layers - 1)
        def _():
            hop(0, c, True).start()

        @pl.when(z > 0)
        def _():
            hop(0, c, False).start()

        across(z, c).start()

    for r in range(1, quads):
        weights(r).wait_recv()
    weights(0).wait()
    product(z)
    for r in range(1, slices):
        columns(z, r).start()
    kept = pltpu.make_async_copy(hidden.at[z, j], hid_out.at[me], own.at[3])
    kept.start()
    for r in range(slices):
        rows(r).start()

    for sent in range(layers - 1):
        for c in range(quads):

            @pl.when(z > sent)
            def _():
                hop_here(sent, c, True).wait_recv()
                across(z - sent - 1, c).start()

            @pl.when((z > sent) & (z < layers - 1))
            def _():
                hop(sent + 1, c, True).start()

            @pl.when(z + sent + 1 < layers)
            def _():
                hop_here(sent, c, False).wait_recv()
                across(z + sent + 1, c).start()

            @pl.when((z + sent + 1 < layers) & (z > 0))
            def _():
                hop(sent + 1, c, False).start()

        @pl.when(z > sent)
        def _():
            product(z - sent - 1)
            for r in range(slices):
                columns(z - sent - 1, r).start()

        @pl.when(z + sent + 1 < layers)
        def _():
            product(z + sent + 1)
            for r in range(slices):
                columns(z + sent + 1, r).start()

    for c in range(quads):
        for r in range(1, layers):
            term(c, r).wait_send()
        for layer in range(layers):
            across(layer, c).wait_send()
        for sent in range(layers - 1):

            @pl.when((z < layers - 1) & (z >= sent))
            def _():
                hop(sent, c, True).wait_send()

            @pl.when((z > 0) & (z + sent < layers))
            def _():
                hop(sent, c, False).wait_send()

    for r in range(1, quads):
        weights(r).wait_send()
    for r in range(slices):
        passages(r).wait()
        rows(r).wait()
    kept.wait()

    def arrived(r, c):
        target = lax.rem(me + r, devices)
        send_to(
            hidden.at[target // slices, lax.rem(target, slices)],
            hid_out.at[lax.rem(me - r + devices, devices)],
            hid_send.at[r],
            hid_recv.at[r],
            target,
        ).wait()
        return c

    lax.fori_loop(1, devices, arrived, 0)


def outward(devices, slices, dq, dkv, weight):
    layers, quads = devices // slices, slices // 2
    _, _, row_count, lanes = dq.shape
    out_columns = weight.shape[0]
    dma = pltpu.SemaphoreType.DMA
    anywhere = pl.BlockSpec(memory_space=pl.ANY)
    return pl.pallas_call(
        functools.partial(outward_kernel, devices, slices),
        out_shape=(
            jax.ShapeDtypeStruct((slices, row_count, lanes), jnp.float32),
            jax.ShapeDtypeStruct(dkv.shape, dkv.dtype),
            jax.ShapeDtypeStruct((devices, row_count, quads * out_columns), jnp.bfloat16),
        ),
        in_specs=[pl.BlockSpec(memory_space=pltpu.VMEM), anywhere, anywhere],
        out_specs=(anywhere,) * 3,
        scratch_shapes=[
            pltpu.VMEM(dq.shape, dq.dtype),
            pltpu.VMEM((slices, row_count, lanes), jnp.float32),
            pltpu.VMEM((2, layers, slices * row_count, lanes), jnp.bfloat16),
            pltpu.VMEM((quads, out_columns, 2 * lanes), weight.dtype),
            pltpu.VMEM((layers, slices, row_count, quads * out_columns), jnp.bfloat16),
        ]
        + [dma((quads, layers))] * 2
        + [dma((layers, quads))] * 6
        + [dma((quads,))] * 2
        + [dma((slices,))] * 4
        + [dma((devices,))] * 2
        + [dma((4,))],
        compiler_params=pltpu.CompilerParams(
            collective_id=1, has_side_effects=True, vmem_limit_bytes=40 * 2**20
        ),
        cost_estimate=pl.CostEstimate(flops=2 * 2**29, bytes_accessed=60 * 2**20, transcendentals=0),
        name="exchange_out",
    )(dq, dkv, weight)


def finish_kernel(slices, steps, dkv_ref, hidden_ref, gq_ref, dk_ref, dv_ref, out_ref, dq_ref):
    step = pl.program_id(0)
    quads = slices // 2
    layers, width = hidden_ref.shape[0], hidden_ref.shape[-1] // quads
    head, lanes = dkv_ref.shape[-1], gq_ref.shape[-1]
    for h in range(2):
        dk_ref[:, h * head : (h + 1) * head] = dkv_ref[h, 0].astype(jnp.float32)
        dv_ref[:, h * head : (h + 1) * head] = dkv_ref[h, 1].astype(jnp.float32)
    for z in range(layers):

        @pl.when(step == z % steps)
        def _():
            for parity in range(2):
                total = hidden_ref[z, 0, parity].astype(jnp.float32)
                for k in range(1, quads):
                    total += hidden_ref[z, k, parity].astype(jnp.float32)
                for k in range(quads):
                    first = (z * slices + 2 * k + parity) * width
                    out_ref[:, first : first + width] = total[:, k * width : (k + 1) * width]

    @pl.when(step == steps - 1)
    def _():
        for p in range(slices):
            dq_ref[:, p * lanes : (p + 1) * lanes] = gq_ref[p]


def finish(slices, dkv, hidden, summed):
    _, _, span, width = dkv.shape
    layers, quads, _, row_count, part = hidden.shape
    steps = slices // 2
    out = jax.ShapeDtypeStruct((span, slices * width), jnp.float32)
    whole = lambda shape: pl.BlockSpec(shape, lambda s: (0,) * len(shape))
    hidden_shape = (row_count, layers * 2 * part)
    query_shape = (row_count, slices * summed.shape[2])
    return pl.pallas_call(
        functools.partial(finish_kernel, slices, steps),
        out_shape=(
            out,
            out,
            jax.ShapeDtypeStruct(hidden_shape, jnp.float32),
            jax.ShapeDtypeStruct(query_shape, jnp.float32),
        ),
        grid=(steps,),
        in_specs=[
            pl.BlockSpec((2, 2, span, width), lambda s: (s, 0, 0, 0)),
            whole(hidden.shape),
            whole(summed.shape),
        ],
        out_specs=(
            pl.BlockSpec((span, 2 * width), lambda s: (0, s)),
            pl.BlockSpec((span, 2 * width), lambda s: (0, s)),
            whole(hidden_shape),
            whole(query_shape),
        ),
        compiler_params=pltpu.CompilerParams(vmem_limit_bytes=58 * 2**20),
        cost_estimate=pl.CostEstimate(flops=0, bytes_accessed=8 * 2**20, transcendentals=0),
        name="finish",
    )(dkv, hidden, summed)


def on_device(queries, grad_out, attn_out, log_sum, keys, values, proj_weight, attend, qlen):
    row_count, columns = queries.shape
    head_count = log_sum.shape[0]
    slices = head_count // GROUP
    span = keys.shape[0]
    devices = lax.axis_size("psg")
    layers = devices // slices
    me = lax.axis_index("psg")
    lanes = GROUP * ATTN_WIDTH
    wide = GROUP * row_count
    run = functools.partial(exchange, devices=devices, slices=slices)

    products = grad_out.astype(jnp.float32) * attn_out.astype(jnp.float32)
    delta = jnp.sum(products.reshape(row_count, head_count, ATTN_WIDTH), axis=2).T
    ld = jnp.stack([log_sum * LOG2_E, delta])
    ld = ld.reshape(2, slices, wide).transpose(1, 0, 2)
    if slices > 1:
        qg, ld, kv = inward(devices, slices, queries, grad_out, ld, keys, values)
    else:
        kv = jnp.stack([keys, values])[None]
        qg = jnp.stack([queries, grad_out])[None]
        qg, ld = run("exchange_in", 0, parts=[("cast", qg), ("cast", ld)])

    out_dtype = jnp.bfloat16 if slices > 1 else jnp.float32
    dkv, dq = attention(attend, qlen, kv, qg, ld, out_dtype)

    dq = dq.reshape(layers, slices, row_count, lanes)
    out_columns = proj_weight.shape[0]
    if slices > 1:
        summed, dkv, hidden = outward(devices, slices, dq, dkv, proj_weight)
        hidden = hidden.reshape(layers, slices // 2, 2, row_count, slices // 2 * out_columns)
        grad_keys, grad_values, hidden, grad_query = finish(slices, dkv, hidden, summed)
    else:
        (dq,) = run("exchange_terms", 1, parts=[("all", dq)])
        summed = jnp.sum(dq.astype(jnp.float32), axis=0)
        low = summed.astype(jnp.bfloat16).reshape(row_count, lanes)
        all_low = lax.all_gather(low, "psg", axis=0, tiled=True)
        hidden = dot(all_low, proj_weight, NT)
        hidden = lax.all_to_all(hidden.reshape(devices, row_count, out_columns), "psg", 0, 0)
        hidden = hidden.transpose(1, 0, 2).reshape(row_count, devices * out_columns)
        grad_keys, grad_values = dkv[0, 0], dkv[0, 1]
        grad_query = summed.reshape(row_count, columns)
    grad_hidden = lax.psum(hidden, "qry")
    return (grad_query, grad_keys, grad_values, grad_hidden)


def solution(mesh):
    in_specs = (
        P("psg", "qry"),
        P("psg", "qry"),
        P("psg", "qry"),
        P("qry", "psg"),
        P("psg", "qry"),
        P("psg", "qry"),
        P("psg", "qry"),
        P(),
        P(),
    )
    out_specs = (P("psg", "qry"), P("psg", "qry"), P("psg", "qry"), P("psg", None))
    return jax.shard_map(
        on_device, mesh=mesh, in_specs=in_specs, out_specs=out_specs, check_vma=False
    )
```

profile of v0, /device:TPU:0, one launch (start us, length us, event | category | flops | bytes accessed | tf_op | source)
XLA Modules:
  0.0 159.0 jit_solution(10117522152454251637)
XLA Ops:
  0.6 0.7 broadcast_multiply_fusion
  1.4 0.1 stack.9
  1.4 1.1 multiply_bitcast_fusion
  2.5 0.1 copy.14
  2.6 0.2 reduce_sum.9
  2.8 0.1 copy.13
  2.9 0.1 stack.10
  3.0 0.6 maximum_bitcast_fusion.refs_2_
  3.6 57.1 %exchange_in.1 = (bf16[32,2,32,512]{3,2,1,0:T(8,128)(2,1)}, f32[32,2,128]{2,1,0:T(2,128)}, bf16[8,2,512,128]{3,2,1,0:T(8,128)(2,1)}) custom-call(bf16[32,4096]{1,0:T(8,128)(2,1)} %refs_0_.1, bf16[32,4096]{1,0:T(8,128)(2,1)} %refs_1_.1, f32[8,2,128]{2,1,0:T(2,128)} %maximum_bitcast_fusion.refs_2_, bf16[512,1024]{1,0:T(8,128)(2,1)} %refs_3_.1, ...), custom_call_target="tpu_custom_call" | custom-call | bytes 62914560 | tf_op jit(solution)/shard_map/exchange_in/pallas_call | solution.py:451
  60.8 0.0 copy-start.3
  60.8 24.2 %attention.1 = (bf16[8,2,512,128]{3,2,1,0:T(8,128)(2,1)}, bf16[32,32,512]{2,1,0:T(8,128)(2,1)}) custom-call(s32[4,16]{1,0:T(4,128)} %attend.1, s32[4]{0:T(128)} %qlen.1, bf16[8,2,512,128]{3,2,1,0:T(8,128)(2,1)} %get-tuple-element.16.kv_ref, bf16[32,2,32,512]{3,2,1,0:T(8,128)(2,1)} %get-tuple-element.17.qg_ref, f32[32,2,128]{2,1,0:T(2,128)} %get-tuple-element.18.ld_ref), custom_call_target="tpu_custom_call" | custom-call | flops 10737418240 | bytes 16777216 | tf_op jit(solution)/shard_map/attention/pallas_call | solution.py:107
  85.0 0.0 copy-done.3
  85.0 0.0 copy-start.1
  85.0 1.6 copy-done.1
  86.6 0.0 copy-start.4
  86.6 1.2 copy-done.4
  87.8 62.9 %exchange_out.1 = (f32[8,32,512]{2,1,0:T(8,128)S(1)}, bf16[8,2,512,128]{3,2,1,0:T(8,128)(2,1)S(1)}, bf16[32,32,512]{2,1,0:T(8,128)(2,1)S(1)}) custom-call(bf16[4,8,32,512]{3,2,1,0:T(8,128)(2,1)S(1)} %bitcast.9, bf16[8,2,512,128]{3,2,1,0:T(8,128)(2,1)S(1)} %copy-done.1, bf16[128,4096]{1,0:T(8,128)(2,1)S(1)} %copy-done.3), custom_call_target="tpu_custom_call" | custom-call | flops 1073741824 | bytes 62914560 | tf_op jit(solution)/shard_map/exchange_out/pallas_call | solution.py:674
  150.8 0.0 copy-start
  150.8 1.3 copy-done
  152.1 0.0 copy-start.2
  152.1 1.0 copy-done.2
  153.1 0.0 copy-start.5
  153.1 0.8 copy-done.5
  153.9 5.1 %finish.1 = (f32[512,1024]{1,0:T(8,128)}, f32[512,1024]{1,0:T(8,128)}, f32[32,4096]{1,0:T(8,128)}, f32[32,4096]{1,0:T(8,128)}) custom-call(bf16[8,2,512,128]{3,2,1,0:T(8,128)(2,1)} %copy-done, bf16[4,4,2,32,512]{4,3,2,1,0:T(8,128)(2,1)} %bitcast.8, f32[8,32,512]{2,1,0:T(8,128)} %copy-done.5), custom_call_target="tpu_custom_call" | custom-call | bytes 8388608 | tf_op jit(solution)/shard_map/finish/pallas_call | solution.py:738
Async XLA Ops:
  60.8 24.2 %copy-start.3 = (bf16[128,4096]{1,0:T(8,128)(2,1)S(1)}, bf16[128,4096]{1,0:T(8,128)(2,1)}, u32[]{:S(2)}) copy-start(bf16[128,4096]{1,0:T(8,128)(2,1)} %w_ref.1) | copy-start | bytes 3145732
  85.0 1.6 %copy-start.1 = (bf16[8,2,512,128]{3,2,1,0:T(8,128)(2,1)S(1)}, bf16[8,2,512,128]{3,2,1,0:T(8,128)(2,1)}, u32[]{:S(2)}) copy-start(bf16[8,2,512,128]{3,2,1,0:T(8,128)(2,1)} %get-tuple-element.20.dkv_ref) | copy-start | bytes 6291460
  86.6 1.2 copy-start.4
  150.8 1.3 copy-start
  152.1 1.0 copy-start.2
  153.1 0.8 copy-start.5
where the time goes:
time: 161 us; the launch traced here: 159 us
  Pallas kernels  149 us (93%)
  local copies, waits for them, and re-layouts  6.26 us (4%)
  other arithmetic  2.63 us (2%)
    pallas_call x1, Pallas kernels, outward(): pl.pallas_call(functools.partial(outward_kernel, devices, slices), out_sh...  62.9 us
    pallas_call x1, Pallas kernels, inward(): pl.pallas_call(functools.partial(inward_kernel, devices, slices), out_sha...  57.1 us
    pallas_call x1, Pallas kernels, attention(): pl.pallas_call(functools.partial(attention_kernel, blocks, tile_count, pe...  24.2 us
    unnamed x13, local copies, waits for them, and re-layouts  6.03 us
    pallas_call x1, Pallas kernels, finish(): pl.pallas_call(functools.partial(finish_kernel, slices, steps), out_shape...  5.12 us

commit v1 on v0

--- a/solution.py
+++ b/solution.py
@@ -46,10 +46,11 @@
     dv_acc[...] = jnp.zeros_like(dv_acc)
     key_rows_t = kv_ref[0, 0].T
 
-    def visit(tile, carry):
+    def visit(first_tile, tile_total):
         keys, values = kv_ref[0, 0], kv_ref[0, 1]
         dk, dv = None, None
-        for part in range(2):
+        for step in range(2 * tile_total):
+            tile, part = first_tile + step // 2, step % 2
             rows = slice(part * 256, part * 256 + 256)
             first = tile * per_tile + part * per_part
             q = head_rows(qg_ref, first, per_part, 0)
@@ -66,7 +67,6 @@
             dq_acc[tile, :, rows] += dot(key_rows_t, dscore)
         dk_acc[...] += dk
         dv_acc[...] += dv
-        return carry
 
     mine = lax.axis_index("psg")
     mine = mine - lax.rem(mine, blocks) + block
@@ -76,9 +76,14 @@
         hits = attend[question, 0] == mine
         for i in range(1, named):
             hits = hits | (attend[question, i] == mine)
-        first = question * (PADDED_ASK_LEN // TILE)
-        count = jnp.where(hits, qlen[question] // TILE, 0)
-        return lax.fori_loop(first, first + count, visit, carry)
+        most = PADDED_ASK_LEN // TILE
+        for count in range(1, most + 1):
+
+            @pl.when(hits & (qlen[question] // TILE == count))
+            def _():
+                visit(question * most, count)
+
+        return carry
 
     lax.fori_loop(0, questions, ask, 0)
     dkv_ref[0, 0] = (dk_acc[...] * SCALE).astype(dkv_ref.dtype)
@@ -694,7 +699,7 @@
         + [dma((devices,))] * 2
         + [dma((4,))],
         compiler_params=pltpu.CompilerParams(
-            collective_id=1, has_side_effects=True, vmem_limit_bytes=40 * 2**20
+            collective_id=1, has_side_effects=True, vmem_limit_bytes=58 * 2**20
         ),
         cost_estimate=pl.CostEstimate(flops=2 * 2**29, bytes_accessed=60 * 2**20, transcendentals=0),
         name="exchange_out",

time: 161 us -> 156 us (0.969); the launches traced: 159 us -> 157 us
  local copies, waits for them, and re-layouts: 6.26 us -> 0.33 us
  Pallas kernels: 149 us -> 153 us
    unnamed x13 -> x1, local copies, waits for them, and re-layouts: 6.03 us -> 0.1 us
    pallas_call x1, Pallas kernels: 62.9 us -> 67 us  [outward(): pl.pallas_call(functools.partial(outward_kernel, devices, slices), out_sh...]
where the time goes in v1:
time: 156 us; the launch traced here: 157 us
  Pallas kernels  153 us (98%)
  other arithmetic  2.63 us (2%)
    pallas_call x1, Pallas kernels, outward(): pl.pallas_call(functools.partial(outward_kernel, devices, slices), out_sh...  67 us
    pallas_call x1, Pallas kernels, inward(): pl.pallas_call(functools.partial(inward_kernel, devices, slices), out_sha...  57.1 us
    pallas_call x1, Pallas kernels, attention(): pl.pallas_call(functools.partial(attention_kernel, blocks, tile_count, pe...  23.7 us
    pallas_call x1, Pallas kernels, finish(): pl.pallas_call(functools.partial(finish_kernel, slices, steps), out_shape...  5.15 us

profile of v1, /device:TPU:0, one launch (start us, length us, event | category | flops | bytes accessed | tf_op | source)
XLA Modules:
  0.0 156.7 jit_solution(12758487382780583870)
XLA Ops:
  0.6 0.7 broadcast_multiply_fusion
  1.4 0.1 stack.9
  1.4 1.1 multiply_bitcast_fusion
  2.5 0.1 copy.14
  2.6 0.2 reduce_sum.9
  2.8 0.1 copy.13
  2.9 0.1 stack.10
  3.0 0.6 maximum_bitcast_fusion.refs_2_
  3.6 57.1 %exchange_in.1 = (bf16[32,2,32,512]{3,2,1,0:T(8,128)(2,1)}, f32[32,2,128]{2,1,0:T(2,128)}, bf16[8,2,512,128]{3,2,1,0:T(8,128)(2,1)}) custom-call(bf16[32,4096]{1,0:T(8,128)(2,1)} %refs_0_.1, bf16[32,4096]{1,0:T(8,128)(2,1)} %refs_1_.1, f32[8,2,128]{2,1,0:T(2,128)} %maximum_bitcast_fusion.refs_2_, bf16[512,1024]{1,0:T(8,128)(2,1)} %refs_3_.1, ...), custom_call_target="tpu_custom_call" | custom-call | bytes 62914560 | tf_op jit(solution)/shard_map/exchange_in/pallas_call | solution.py:456
  60.8 23.7 %attention.1 = (bf16[8,2,512,128]{3,2,1,0:T(8,128)(2,1)}, bf16[32,32,512]{2,1,0:T(8,128)(2,1)}) custom-call(s32[4,16]{1,0:T(4,128)} %attend.1, s32[4]{0:T(128)} %qlen.1, bf16[8,2,512,128]{3,2,1,0:T(8,128)(2,1)} %get-tuple-element.16.kv_ref, bf16[32,2,32,512]{3,2,1,0:T(8,128)(2,1)} %get-tuple-element.17.qg_ref, f32[32,2,128]{2,1,0:T(2,128)} %get-tuple-element.18.ld_ref), custom_call_target="tpu_custom_call" | custom-call | flops 10737418240 | bytes 16777216 | tf_op jit(solution)/shard_map/attention/pallas_call | solution.py:112
  84.5 67.0 %exchange_out.1 = (f32[8,32,512]{2,1,0:T(8,128)}, bf16[8,2,512,128]{3,2,1,0:T(8,128)(2,1)}, bf16[32,32,512]{2,1,0:T(8,128)(2,1)}) custom-call(bf16[4,8,32,512]{3,2,1,0:T(8,128)(2,1)} %bitcast.10, bf16[8,2,512,128]{3,2,1,0:T(8,128)(2,1)} %get-tuple-element.20.dkv_ref, bf16[128,4096]{1,0:T(8,128)(2,1)} %w_ref.1), custom_call_target="tpu_custom_call" | custom-call | flops 1073741824 | bytes 62914560 | tf_op jit(solution)/shard_map/exchange_out/pallas_call | solution.py:679
  151.5 5.1 %finish.1 = (f32[512,1024]{1,0:T(8,128)}, f32[512,1024]{1,0:T(8,128)}, f32[32,4096]{1,0:T(8,128)}, f32[32,4096]{1,0:T(8,128)}) custom-call(bf16[8,2,512,128]{3,2,1,0:T(8,128)(2,1)} %get-tuple-element.21.dkv_ref, bf16[4,4,2,32,512]{4,3,2,1,0:T(8,128)(2,1)} %bitcast.9, f32[8,32,512]{2,1,0:T(8,128)} %get-tuple-element.23.gq_ref), custom_call_target="tpu_custom_call" | custom-call | bytes 8388608 | tf_op jit(solution)/shard_map/finish/pallas_call | solution.py:743
